TPU v7x, 32 devices: a whole 2x2x4 slice. The times are simulated.
32 devices in a mesh: gas: 8 (over z, y), space: 4 (over x, core).
Axes of the slice: x: 2, y: 2, z: 4, core: 2. Of those that a mesh axis runs over, the one named last changes fastest.
Arguments:
- particle_amount: bfloat16 [1024, 256, 8, 128], P('gas', 'space'), may hold values from 0 to 1
- section_opacity: bfloat16 [1024, 16], P('gas'), may hold values from 0.0009994507 to 0.0099487305
- species_opacity_factor: float32 [16], replicated, may hold values from 0.05 to 0.5
- absorber_molefraction: float32 [256, 8, 128], P('space'), may hold values from 0 to 1
- scaled_heat_level: float32 [256, 8, 128], P('space'), may hold values from 0.24 to 1.68
- wall_touching_flag: int32 [256, 8, 128], P('space'), may hold values 0 or 1
- fraction_polynomial: float32 [16, 3], replicated, may hold values from 0.05 to 1.35
Outputs:
- divergence: float32 [256, 8, 128], P('space')
- average_radiative_loss: float32 [], replicated
All inputs are finite; a program needn't handle non-finite values. No bound on the sum of `wall_touching_flag` on one device may be relied on, other than what follows from the above.
Results may differ from a plain program's by a relative error of at most 0.0003.
Values sent between devices are 32-bit elements; how exact they have to be, the bound alone decides.
A program may use at most 64 MiB of HBM per device.

v0:
```python
import jax
import jax.numpy as jnp
from jax import lax
from jax.sharding import PartitionSpec as P

SWEEPS = 6
KAPPA_FLOOR = 0.5
WALL_LOSS = 0.5
LAM_LOW = 0.5
LAM_HIGH = 12.0


def with_halo(x, sides, width):
    for axis, dim in sides:
        peers, length = (lax.axis_size(axis), x.shape[dim])
        up = [(i, (i + 1) % peers) for i in range(peers - 1)]
        down = [(j, i) for i, j in up]
        last = lax.slice_in_dim(x, length - width, length, axis=dim)
        leading = lax.slice_in_dim(x, 0, width, axis=dim)
        before = lax.ppermute(last, axis, up)
        after = lax.ppermute(leading, axis, down)
        x = jnp.concatenate([before, x, after], axis=dim)
    return x


def lower(values, dimension):
    border = jnp.zeros_like(lax.slice_in_dim(values, 0, 1, axis=dimension))
    return jnp.concatenate(
        [border, lax.slice_in_dim(values, 0, values.shape[dimension] - 1, axis=dimension)],
        dimension,
    )


def upper(values, dimension):
    border = jnp.zeros_like(lax.slice_in_dim(values, 0, 1, axis=dimension))
    return jnp.concatenate(
        [lax.slice_in_dim(values, 1, values.shape[dimension], axis=dimension), border], dimension
    )


def coupling(paired_total):
    positive = paired_total > 0.0
    return jnp.where(positive, 2.0 / (3.0 * jnp.where(positive, paired_total, 1.0)), 0.0)


def per_device(
    particle_amount,
    section_opacity,
    species_opacity_factor,
    absorber_molefraction,
    scaled_heat_level,
    wall_touching_flag,
    fraction_polynomial,
):
    gas_count = lax.axis_size("gas")
    per_gas = species_opacity_factor.shape[0] // gas_count
    first_gas = lax.axis_index("gas") * per_gas
    width_x = absorber_molefraction.shape[0]
    total_x = width_x * lax.axis_size("space")
    soot_flat = particle_amount.reshape(particle_amount.shape[0], -1)
    summed_all = lax.psum(
        lax.dot_general(
            section_opacity, soot_flat, (((0,), (0,)), ((), ())), preferred_element_type=jnp.float32
        ),
        "gas",
    )
    own_soot = lax.dynamic_slice_in_dim(summed_all, first_gas, per_gas, 0)
    own_soot = own_soot.reshape((per_gas,) + absorber_molefraction.shape)
    strength = lax.dynamic_slice_in_dim(species_opacity_factor, first_gas, per_gas, 0)
    component_lines = lax.dynamic_slice_in_dim(fraction_polynomial, first_gas, per_gas, 0)
    absorption = (
        KAPPA_FLOOR + strength[:, None, None, None] * absorber_molefraction[None] + own_soot
    )
    heat_level_square = scaled_heat_level * scaled_heat_level
    component_fractions = (
        component_lines[:, 0][:, None, None, None]
        + component_lines[:, 1][:, None, None, None] * scaled_heat_level[None]
        + component_lines[:, 2][:, None, None, None] * heat_level_square[None]
    )
    emitted_power = component_fractions * (heat_level_square * heat_level_square)[None]
    base_diag = absorption + WALL_LOSS * wall_touching_flag.astype(jnp.float32)[None]
    halo_depth = 1
    widened = with_halo(jnp.stack([absorption, base_diag]), (("space", 2),), halo_depth)
    wide_abs = widened[0]
    inner_abs = wide_abs[:, 1:-1]
    couple = (
        coupling(inner_abs + wide_abs[:, :-2]),
        coupling(inner_abs + wide_abs[:, 2:]),
        coupling(inner_abs + lower(inner_abs, 2)),
        coupling(inner_abs + upper(inner_abs, 2)),
        coupling(inner_abs + lower(inner_abs, 3)),
        coupling(inner_abs + upper(inner_abs, 3)),
    )
    diagonal = widened[1][:, 1:-1]
    for weight_face in couple:
        diagonal = diagonal + weight_face
    rows_wide = width_x + 2 * halo_depth - 2
    global_row = (
        lax.axis_index("space") * width_x - halo_depth + 1 + jnp.arange(rows_wide, dtype=jnp.int32)
    )
    inside = ((global_row >= 0) & (global_row < total_x)).astype(jnp.float32)[None, :, None, None]
    centre = (LAM_HIGH + LAM_LOW) / 2.0
    spread_half = (LAM_HIGH - LAM_LOW) / 2.0
    ratio_sigma = centre / spread_half
    residual = absorption * emitted_power
    direction = residual / centre
    iterate = jnp.zeros_like(residual)
    ratio_now = 1.0 / ratio_sigma
    for sweep_index in range(SWEEPS):
        residual, direction = (residual, with_halo(direction, (("space", 1),), 1))
        span_rows = direction.shape[1]
        middle = direction[:, 1:-1]
        applied = diagonal * middle
        beside = (
            direction[:, :-2],
            direction[:, 2:],
            lower(middle, 2),
            upper(middle, 2),
            lower(middle, 3),
            upper(middle, 3),
        )
        for weight_face, neighbour in zip(couple, beside):
            applied = applied - weight_face * neighbour
        inner_start = (span_rows - width_x) // 2
        iterate = iterate + direction[:, inner_start : inner_start + width_x]
        residual = (residual - applied) * inside
        ratio_next = 1.0 / (2.0 * ratio_sigma - ratio_now)
        direction = (
            ratio_next * ratio_now * middle + 2.0 * ratio_next / spread_half * residual
        ) * inside
        ratio_now = ratio_next
    gas_terms = absorption * (emitted_power - iterate)
    divergence = lax.psum(jnp.sum(gas_terms, axis=0), "gas")
    cell_count = total_x * absorber_molefraction.shape[1] * absorber_molefraction.shape[2]
    average_radiative_loss = lax.psum(jnp.sum(divergence), "space") / cell_count
    return (divergence, average_radiative_loss)


def solution(mesh):
    return jax.shard_map(
        per_device,
        mesh=mesh,
        in_specs=(
            P("gas", "space", None, None),
            P("gas", None),
            P(),
            P("space", None, None),
            P("space", None, None),
            P("space", None, None),
            P(),
        ),
        out_specs=(P("space", None, None), P()),
        check_vma=False,
    )
```

profile of v0, /device:TPU:0, one launch (start us, length us, event | category | flops | bytes accessed | tf_op | source)
XLA Modules:
  0.0 324.8 jit_solution(6322552649570124776)
XLA Ops:
  7.9 16.8 %fusion = f32[16,65536]{1,0:T(8,128)} fusion(bf16[128,16]{0,1:T(8,128)(2,1)S(1)} %copy-done, bf16[16,8,512,128]{3,2,1,0:T(8,128)(2,1)} %bitcast.31), kind=kOutput, calls=%fused_computation | convolution fusion | flops 268435456 | bytes 20975616 | tf_op jit(solution)/shard_map/dot_general | solution.py:62
  25.7 158.1 %all-reduce.27.cloned.1.call-done = f32[16,65536]{1,0:T(8,128)} async-done(((f32[16,65536]{1,0:T(8,128)}), f32[16,65536]{1,0:T(8,128)}) %all-reduce.27.cloned.1.call-update) | async-done | bytes 4194320 | tf_op jit(solution)/shard_map/psum | solution.py:61
  183.8 1.8 dynamic-slice_bitcast_fusion
  186.3 1.7 collective-permute-start
  188.0 1.3 collective-permute-start.1
  189.3 4.3 %collective-permute-start.2 = (f32[2,1,8,128]{3,2,1,0:T(8,128)S(1)}, f32[2,1,8,128]{3,2,1,0:T(8,128)S(1)}, u32[]{:S(2)}, u32[]{:S(2)}) collective-permute-start(f32[2,1,8,128]{3,2,1,0:T(8,128)S(1)} %get-tuple-element.47), channel_id=1, source_target_pairs={{0,1},{1,2},{2,3},{4,5},{5,6},{6,7},{8,9},{9,10},{10,11},{12,13},{... | collective-permute-start | bytes 24584 | tf_op jit(solution)/shard_map/ppermute | solution.py:20
  193.7 1.5 collective-permute-start.3
  195.6 2.4 collective-permute-done.3
  198.0 1.6 add_multiply_fusion.3
  199.8 4.3 %collective-permute-start.4 = (f32[2,1,8,128]{3,2,1,0:T(8,128)S(1)}, f32[2,1,8,128]{3,2,1,0:T(8,128)S(1)}, u32[]{:S(2)}, u32[]{:S(2)}) collective-permute-start(f32[2,1,8,128]{3,2,1,0:T(8,128)S(1)} %get-tuple-element.41), channel_id=1, source_target_pairs={{0,1},{1,2},{2,3},{4,5},{5,6},{6,7},{8,9},{9,10},{10,11},{12,13},{... | collective-permute-start | bytes 24584 | tf_op jit(solution)/shard_map/ppermute | solution.py:20
  205.5 1.7 collective-permute-done.5
  208.0 3.8 %collective-permute-start.6 = (f32[2,1,8,128]{3,2,1,0:T(8,128)S(1)}, f32[2,1,8,128]{3,2,1,0:T(8,128)S(1)}, u32[]{:S(2)}, u32[]{:S(2)}) collective-permute-start(f32[2,1,8,128]{3,2,1,0:T(8,128)S(1)} %get-tuple-element.35), channel_id=1, source_target_pairs={{0,1},{1,2},{2,3},{4,5},{5,6},{6,7},{8,9},{9,10},{10,11},{12,13},{... | collective-permute-start | bytes 24584 | tf_op jit(solution)/shard_map/ppermute | solution.py:20
  213.2 1.7 collective-permute-done.7
  216.2 3.8 %collective-permute-start.8 = (f32[2,1,8,128]{3,2,1,0:T(8,128)S(1)}, f32[2,1,8,128]{3,2,1,0:T(8,128)S(1)}, u32[]{:S(2)}, u32[]{:S(2)}) collective-permute-start(f32[2,1,8,128]{3,2,1,0:T(8,128)S(1)} %get-tuple-element.29), channel_id=1, source_target_pairs={{0,1},{1,2},{2,3},{4,5},{5,6},{6,7},{8,9},{9,10},{10,11},{12,13},{... | collective-permute-start | bytes 24584 | tf_op jit(solution)/shard_map/ppermute | solution.py:20
  220.0 1.3 collective-permute-start.9
  221.4 1.7 collective-permute-done.9
  223.1 2.1 add_multiply_fusion
  225.4 3.8 %collective-permute-start.10 = (f32[2,1,8,128]{3,2,1,0:T(8,128)S(1)}, f32[2,1,8,128]{3,2,1,0:T(8,128)S(1)}, u32[]{:S(2)}, u32[]{:S(2)}) collective-permute-start(f32[2,1,8,128]{3,2,1,0:T(8,128)S(1)} %get-tuple-element.23), channel_id=1, source_target_pairs={{0,1},{1,2},{2,3},{4,5},{5,6},{6,7},{8,9},{9,10},{10,11},{12,13},{... | collective-permute-start | bytes 24584 | tf_op jit(solution)/shard_map/ppermute | solution.py:20
  230.6 1.7 collective-permute-done.11
  232.3 3.9 %fusion.77 = f32[64,8,128]{2,1,0:T(8,128)} fusion(f32[2,64,8,128]{3,2,1,0:T(8,128)S(1)} %get-tuple-element.10, f32[2,64,8,127]{3,2,1,0:T(8,128)S(1)} %get-tuple-element.28, f32[2,64,8,128]{3,2,1,0:T(8,128)S(1)} %get-tuple-element.7, f32[2,64,8,127]{3,2,1,0:T(8,128)S(1)} %get-tuple-element.27, f32[2,64,8,128]{3,2,1,0:T(8,128)S(1)} %get-tuple-element.6, ...), kind=kLoop, calls=%fused_computation.113 | loop fusion | flops 13172736 | bytes 16548128 | tf_op jit(solution)/shard_map/reduce_sum | solution.py:133
  236.2 70.4 %all-reduce.29.cloned.1.call-done = f32[64,8,128]{2,1,0:T(8,128)} async-done(((f32[64,8,128]{2,1,0:T(8,128)}), f32[64,8,128]{2,1,0:T(8,128)}) %all-reduce.29.cloned.1.call-update) | async-done | bytes 262160 | tf_op jit(solution)/shard_map/psum | solution.py:133
  306.6 1.6 reduce_sum.19
  308.2 6.3 %psum.23 = f32[]{:T(128)} all-reduce(f32[]{:T(128)} %reduce_sum.19), channel_id=1, replica_groups=mesh['gas'=8,'space'=4] {'space'}, use_global_device_ids=true, to_apply=%region_4.5 | all-reduce | flops 1 | bytes 8 | tf_op jit(solution)/shard_map/psum | solution.py:135
  315.2 1.7 copy.26
  (56 shorter events, 9.5 us)
Async XLA Ops:
  7.2 0.7 copy-start
  7.2 176.6 %all-reduce.27.cloned.1.call-start = ((), (), s32[]{:S(2)}) async-start(), calls=%async_computation | async-start | bytes 8388608 | tf_op jit(solution)/shard_map/psum | solution.py:61
  24.6 0.7 copy-start.5
  24.6 0.7 copy-start.4
  24.6 1.0 copy-start.3
  24.6 1.1 copy-start.1
  24.6 160.9 %copy-start.2 = (f32[64,8,128]{2,1,0:T(8,128)S(1)}, f32[64,8,128]{2,1,0:T(8,128)}, u32[]{:S(2)}) copy-start(f32[64,8,128]{2,1,0:T(8,128)} %param.10) | copy-start | bytes 786436
  24.7 281.9 %all-reduce.29.cloned.1.call-start = ((), (), s32[]{:S(2)}) async-start(), calls=%async_computation.1 | async-start | bytes 524288 | tf_op jit(solution)/shard_map/psum | solution.py:133
  186.3 8.8 %collective-permute-start = (f32[2,2,1,8,128]{4,3,2,1,0:T(8,128)S(1)}, f32[2,2,1,8,128]{4,3,2,1,0:T(8,128)S(1)}, u32[]{:S(2)}, u32[]{:S(2)}) collective-permute-start(f32[2,2,1,8,128]{4,3,2,1,0:T(8,128)S(1)} %get-tuple-element.17), channel_id=1, source_target_pairs={{0,1},{1,2},{2,3},{4,5},{5,6},{6,7},{8,9},{9,10},{10,11},{12,13},{... | collective-permute-start | bytes 49160 | tf_op jit(solution)/shard_map/ppermute | solution.py:20
  188.0 7.1 %collective-permute-start.1 = (f32[2,2,1,8,128]{4,3,2,1,0:T(8,128)S(1)}, f32[2,2,1,8,128]{4,3,2,1,0:T(8,128)S(1)}, u32[]{:S(2)}, u32[]{:S(2)}) collective-permute-start(f32[2,2,1,8,128]{4,3,2,1,0:T(8,128)S(1)} %get-tuple-element.18), channel_id=1, source_target_pairs={{1,0},{2,1},{3,2},{5,4},{6,5},{7,6},{9,8},{10,9},{11,10},{13,12},{... | collective-permute-start | bytes 49160 | tf_op jit(solution)/shard_map/ppermute | solution.py:21
  189.3 6.3 %collective-permute-start.2 = (f32[2,1,8,128]{3,2,1,0:T(8,128)S(1)}, f32[2,1,8,128]{3,2,1,0:T(8,128)S(1)}, u32[]{:S(2)}, u32[]{:S(2)}) collective-permute-start(f32[2,1,8,128]{3,2,1,0:T(8,128)S(1)} %get-tuple-element.47), channel_id=1, source_target_pairs={{0,1},{1,2},{2,3},{4,5},{5,6},{6,7},{8,9},{9,10},{10,11},{12,13},{... | collective-permute-start | bytes 24584 | tf_op jit(solution)/shard_map/ppermute | solution.py:20
  193.7 4.3 %collective-permute-start.3 = (f32[2,1,8,128]{3,2,1,0:T(8,128)S(1)}, f32[2,1,8,128]{3,2,1,0:T(8,128)S(1)}, u32[]{:S(2)}, u32[]{:S(2)}) collective-permute-start(f32[2,1,8,128]{3,2,1,0:T(8,128)S(1)} %get-tuple-element.48), channel_id=1, source_target_pairs={{1,0},{2,1},{3,2},{5,4},{6,5},{7,6},{9,8},{10,9},{11,10},{13,12},{... | collective-permute-start | bytes 24584 | tf_op jit(solution)/shard_map/ppermute | solution.py:21
  199.8 5.7 %collective-permute-start.4 = (f32[2,1,8,128]{3,2,1,0:T(8,128)S(1)}, f32[2,1,8,128]{3,2,1,0:T(8,128)S(1)}, u32[]{:S(2)}, u32[]{:S(2)}) collective-permute-start(f32[2,1,8,128]{3,2,1,0:T(8,128)S(1)} %get-tuple-element.41), channel_id=1, source_target_pairs={{0,1},{1,2},{2,3},{4,5},{5,6},{6,7},{8,9},{9,10},{10,11},{12,13},{... | collective-permute-start | bytes 24584 | tf_op jit(solution)/shard_map/ppermute | solution.py:20
  204.1 3.1 collective-permute-start.5
  208.0 5.2 %collective-permute-start.6 = (f32[2,1,8,128]{3,2,1,0:T(8,128)S(1)}, f32[2,1,8,128]{3,2,1,0:T(8,128)S(1)}, u32[]{:S(2)}, u32[]{:S(2)}) collective-permute-start(f32[2,1,8,128]{3,2,1,0:T(8,128)S(1)} %get-tuple-element.35), channel_id=1, source_target_pairs={{0,1},{1,2},{2,3},{4,5},{5,6},{6,7},{8,9},{9,10},{10,11},{12,13},{... | collective-permute-start | bytes 24584 | tf_op jit(solution)/shard_map/ppermute | solution.py:20
  211.8 3.1 collective-permute-start.7
  216.2 5.2 %collective-permute-start.8 = (f32[2,1,8,128]{3,2,1,0:T(8,128)S(1)}, f32[2,1,8,128]{3,2,1,0:T(8,128)S(1)}, u32[]{:S(2)}, u32[]{:S(2)}) collective-permute-start(f32[2,1,8,128]{3,2,1,0:T(8,128)S(1)} %get-tuple-element.29), channel_id=1, source_target_pairs={{0,1},{1,2},{2,3},{4,5},{5,6},{6,7},{8,9},{9,10},{10,11},{12,13},{... | collective-permute-start | bytes 24584 | tf_op jit(solution)/shard_map/ppermute | solution.py:20
  220.0 3.1 collective-permute-start.9
  225.4 5.2 %collective-permute-start.10 = (f32[2,1,8,128]{3,2,1,0:T(8,128)S(1)}, f32[2,1,8,128]{3,2,1,0:T(8,128)S(1)}, u32[]{:S(2)}, u32[]{:S(2)}) collective-permute-start(f32[2,1,8,128]{3,2,1,0:T(8,128)S(1)} %get-tuple-element.23), channel_id=1, source_target_pairs={{0,1},{1,2},{2,3},{4,5},{5,6},{6,7},{8,9},{9,10},{10,11},{12,13},{... | collective-permute-start | bytes 24584 | tf_op jit(solution)/shard_map/ppermute | solution.py:20
  229.2 3.1 collective-permute-start.11
Sparse Core Ops, SparseCore 0:
  24.8 158.9 all-reduce.26
  236.3 70.2 all-reduce.28
where the time goes:
time: 325 us
  waiting for transfers between devices  238 us (73%)
  starting transfers between devices  29.9 us (9%)
  matrix products  16.8 us (5%)
  between operations  16.2 us (5%)
  other arithmetic  11.4 us (4%)
  local copies, waits for them, and re-layouts  6.74 us (2%)
  blocking collectives  6.27 us (2%)
    psum x1, waiting for transfers between devices, per_device(): lax.psum(lax.dot_general(section_opacity, soot_flat, (((0,), (0,)), ((),...  158 us
    psum x1, waiting for transfers between devices, per_device(): divergence = lax.psum(jnp.sum(gas_terms, axis=0), 'gas')  70.4 us
    ppermute x6, starting transfers between devices, with_halo(): before = lax.ppermute(last, axis, up)  21.9 us
    dot_general x1, matrix products, per_device(): lax.dot_general(section_opacity, soot_flat, (((0,), (0,)), ((), ())), pre...  16.8 us
    ppermute x6, waiting for transfers between devices, with_halo(): after = lax.ppermute(leading, axis, down)  9.07 us
    ppermute x6, starting transfers between devices, with_halo(): after = lax.ppermute(leading, axis, down)  7.93 us
  transfers between devices with their start and end apart: 14, of which 7 were waited for; matrix products, arithmetic and copies ran while one was open for 0% of the time, Pallas kernels for 0%

commit v1 on v0

--- a/solution.py
+++ b/solution.py
@@ -58,11 +58,17 @@
     width_x = absorber_molefraction.shape[0]
     total_x = width_x * lax.axis_size("space")
     soot_flat = particle_amount.reshape(particle_amount.shape[0], -1)
-    summed_all = lax.psum(
-        lax.dot_general(
-            section_opacity, soot_flat, (((0,), (0,)), ((), ())), preferred_element_type=jnp.float32
+    summed_all = jnp.sum(
+        lax.all_gather(
+            lax.dot_general(
+                section_opacity,
+                soot_flat,
+                (((0,), (0,)), ((), ())),
+                preferred_element_type=jnp.float32,
+            ),
+            "gas",
         ),
-        "gas",
+        axis=0,
     )
     own_soot = lax.dynamic_slice_in_dim(summed_all, first_gas, per_gas, 0)
     own_soot = own_soot.reshape((per_gas,) + absorber_molefraction.shape)

time: 325 us -> 821 us (2.53)
  waiting for transfers between devices: 238 us -> 720 us
  other arithmetic: 11.4 us -> 25.4 us
    all_gather x0 -> x1, waiting for transfers between devices: none -> 640 us  [per_device(): lax.all_gather(lax.dot_general(section_opacity, soot_flat, (((0,), (0,)),...]
    psum x1 -> x0, waiting for transfers between devices: 158 us -> none  [per_device(): lax.psum(lax.dot_general(section_opacity, soot_flat, (((0,), (0,)), ((),...]
    reduce_sum x0 -> x1, other arithmetic: none -> 14.1 us  [per_device(): jnp.sum(lax.all_gather(lax.dot_general(section_opacity, soot_flat, (((0,)...]
where the time goes in v1:
time: 821 us
  waiting for transfers between devices  720 us (88%)
  starting transfers between devices  29.9 us (4%)
  other arithmetic  25.4 us (3%)
  matrix products  16.8 us (2%)
  between operations  16.2 us (2%)
    all_gather x1, waiting for transfers between devices, per_device(): lax.all_gather(lax.dot_general(section_opacity, soot_flat, (((0,), (0,)),...  640 us
    psum x1, waiting for transfers between devices, per_device(): divergence = lax.psum(jnp.sum(gas_terms, axis=0), 'gas')  71.4 us
    ppermute x6, starting transfers between devices, with_halo(): before = lax.ppermute(last, axis, up)  21.9 us
    dot_general x1, matrix products, per_device(): lax.dot_general(section_opacity, soot_flat, (((0,), (0,)), ((), ())), pre...  16.8 us
  transfers between devices with their start and end apart: 14, of which 7 were waited for; matrix products, arithmetic and copies ran while one was open for 0% of the time, Pallas kernels for 0%

profile of v1, /device:TPU:0, one launch (start us, length us, event | category | flops | bytes accessed | tf_op | source)
XLA Modules:
  0.0 820.8 jit_solution(6161626468525109135)
XLA Ops:
  7.9 16.8 %fusion = f32[16,65536]{1,0:T(8,128)} fusion(bf16[128,16]{0,1:T(8,128)(2,1)S(1)} %copy-done, bf16[16,8,512,128]{3,2,1,0:T(8,128)(2,1)} %bitcast.33), kind=kOutput, calls=%fused_computation | convolution fusion | flops 268435456 | bytes 20975616 | tf_op jit(solution)/shard_map/dot_general | solution.py:63
  25.8 639.5 %all-gather.3.cloned.1.call-done = f32[128,65536]{1,0:T(8,128)} async-done(((f32[16,65536]{1,0:T(8,128)}), f32[128,65536]{1,0:T(8,128)}) %all-gather.3.cloned.1.call-update) | async-done | bytes 33554448 | tf_op jit(solution)/shard_map/all_gather | solution.py:62
  665.3 14.1 %reduce_sum.27 = f32[16,65536]{1,0:T(8,128)} reduce(f32[8,16,65536]{2,1,0:T(8,128)} %bitcast.32, f32[]{:T(128)} %constant.8.clone.1), dimensions={0}, to_apply=%region_0.0 | reduce | flops 7340032 | bytes 37748740 | tf_op jit(solution)/shard_map/reduce_sum | solution.py:61
  679.3 1.8 dynamic-slice_bitcast_fusion
  681.9 1.7 collective-permute-start
  683.6 1.3 collective-permute-start.1
  684.9 4.3 collective-permute-start.2
  689.2 1.5 collective-permute-start.3
  691.2 2.4 collective-permute-done.3
  693.5 1.6 add_multiply_fusion.3
  695.2 4.3 collective-permute-start.4
  701.0 1.6 collective-permute-done.5
  703.3 3.8 collective-permute-start.6
  708.6 1.6 collective-permute-done.7
  711.3 3.8 collective-permute-start.8
  716.7 1.6 collective-permute-done.9
  718.3 2.1 add_multiply_fusion
  720.4 3.8 collective-permute-start.10
  725.8 1.6 collective-permute-done.11
  727.4 3.9 fusion.77
  731.2 71.4 %all-reduce.26.cloned.1.call-done = f32[64,8,128]{2,1,0:T(8,128)} async-done(((f32[64,8,128]{2,1,0:T(8,128)}), f32[64,8,128]{2,1,0:T(8,128)}) %all-reduce.26.cloned.1.call-update) | async-done | bytes 262160 | tf_op jit(solution)/shard_map/psum | solution.py:139
  802.6 1.6 reduce_sum.29
  804.2 6.3 psum.15
  811.2 1.7 copy.25
  (59 shorter events, 10.8 us)
Async XLA Ops:
  7.2 0.7 copy-start
  7.2 658.1 %all-gather.3.cloned.1.call-start = ((), (), s32[]{:S(2)}) async-start(), calls=%async_computation.1 | async-start | bytes 37748736 | tf_op jit(solution)/shard_map/all_gather | solution.py:62
  24.7 0.7 copy-start.6
  24.7 0.7 copy-start.5
  24.7 1.0 copy-start.4
  24.7 1.1 copy-start.2
  24.7 777.9 %all-reduce.26.cloned.1.call-start = ((), (), s32[]{:S(2)}) async-start(), calls=%async_computation | async-start | bytes 524288 | tf_op jit(solution)/shard_map/psum | solution.py:139
  665.3 15.8 %copy-start.3 = (f32[64,8,128]{2,1,0:T(8,128)S(1)}, f32[64,8,128]{2,1,0:T(8,128)}, u32[]{:S(2)}) copy-start(f32[64,8,128]{2,1,0:T(8,128)} %param.10) | copy-start | bytes 786436
  681.9 8.8 %collective-permute-start = (f32[2,2,1,8,128]{4,3,2,1,0:T(8,128)S(1)}, f32[2,2,1,8,128]{4,3,2,1,0:T(8,128)S(1)}, u32[]{:S(2)}, u32[]{:S(2)}) collective-permute-start(f32[2,2,1,8,128]{4,3,2,1,0:T(8,128)S(1)} %get-tuple-element.17), channel_id=1, source_target_pairs={{0,1},{1,2},{2,3},{4,5},{5,6},{6,7},{8,9},{9,10},{10,11},{12,13},{... | collective-permute-start | bytes 49160 | tf_op jit(solution)/shard_map/ppermute | solution.py:20
  683.6 7.1 collective-permute-start.1
  684.9 6.2 collective-permute-start.2
  689.2 4.3 collective-permute-start.3
  695.2 5.8 collective-permute-start.4
  699.5 3.1 collective-permute-start.5
  703.3 5.4 collective-permute-start.6
  707.1 3.1 collective-permute-start.7
  711.3 5.4 collective-permute-start.8
  715.2 3.1 collective-permute-start.9
  720.4 5.4 collective-permute-start.10
  724.3 3.1 collective-permute-start.11
  727.4 85.5 %copy-start.1 = (bf16[128,16]{0,1:T(8,128)(2,1)S(1)}, bf16[128,16]{0,1:T(8,128)(2,1)}, u32[]{:S(2)}) copy-start(bf16[128,16]{0,1:T(8,128)(2,1)} %param.8) | copy-start | bytes 12292
Sparse Core Ops, SparseCore 0:
  24.8 640.4 all-gather.2
  731.4 71.2 all-reduce.25
